TPU v7x, 256 devices: a whole 4x4x8 slice. The times are simulated.
256 devices in a mesh: dp: 32 (over x, y, core), ffn: 8 (over z).
Axes of the slice: x: 4, y: 4, z: 8, core: 2. Of those that a mesh axis runs over, the one named last changes fastest.
Arguments:
- resid: bfloat16 [1024, 8192], P('dp', 'ffn'), may hold values from -6 to 6
- attn_out: bfloat16 [1024, 8192], P('dp', 'ffn'), may hold values from -6 to 6
- norm_gain: float32 [8192], P('ffn'), may hold values from 0.25 to 1.75
- w_gate: bfloat16 [8192, 14784], P('ffn', 'dp'), may hold values from -0.0625 to 0.0625
- w_up: bfloat16 [8192, 14784], P('ffn', 'dp'), may hold values from -0.0625 to 0.0625
- w_down: bfloat16 [14784, 8192], P('dp', 'ffn'), may hold values from -0.046875 to 0.046875
- w_head: bfloat16 [8192, 18], P('ffn'), may hold values from -0.0625 to 0.0625
- actions: int32 [1024], P('dp'), may hold values from 0 to 17
- step_index: int32 [1024], P('dp'), may hold values from 0 to 63
- trace_code: int32 [1024], P('dp'), may hold values from 0 to 8
- targets: float32 [1024], P('dp'), may hold values from -6 to 6
Outputs:
- grad_gate: float32 [8192, 14784], P('ffn', 'dp')
- grad_up: float32 [8192, 14784], P('ffn', 'dp')
- grad_down: float32 [14784, 8192], P('dp', 'ffn')
- grad_head: float32 [8192, 18], P('ffn')
- loss: float32 [], replicated
All inputs are finite; a program needn't handle non-finite values.
Results may differ from a plain program's by a relative error of at most 0.0062.
Values may be sent and summed in bfloat16 or wider, within the bound.
A program may use at most 64 MiB of HBM per device.

v0:
```python
import jax
import jax.numpy as jnp
from jax import lax
from jax.sharding import PartitionSpec as P

D = 8192
LEVELS = 8


def body(
    resid,
    attn_out,
    norm_gain,
    w_gate,
    w_up,
    w_down,
    w_head,
    actions,
    step_index,
    trace_code,
    targets,
):
    highest = lax.Precision.HIGHEST
    summed = resid.astype(jnp.float32) + attn_out.astype(jnp.float32)
    square_sums = lax.psum(jnp.sum(summed * summed, axis=1), "ffn")
    normed = (summed * lax.rsqrt(square_sums[:, None] / D + 1e-06) * norm_gain).astype(jnp.bfloat16)
    normed_all = lax.all_gather(normed, "dp", axis=0, tiled=True)
    total_rows = normed_all.shape[0]
    hidden_width = w_gate.shape[1]
    paired = jnp.concatenate([w_gate, w_up], axis=1)
    block = normed_all
    paired_sums = lax.psum_scatter(
        jnp.dot(block, paired, preferred_element_type=jnp.float32),
        "ffn",
        scatter_dimension=0,
        tiled=True,
    )
    gate = paired_sums[:, :hidden_width]
    up_proj = paired_sums[:, hidden_width:]
    hidden = (jax.nn.silu(gate) * up_proj).astype(jnp.bfloat16)
    hidden_all = lax.all_gather(hidden, "ffn", axis=0, tiled=True)
    num_actions = w_head.shape[1]
    critic_head = w_head.astype(jnp.float32)
    one_hot = (actions[:, None] == jnp.arange(num_actions, dtype=jnp.int32)[None, :]).astype(
        jnp.float32
    )
    weight = (
        jnp.power(jnp.float32(0.97), step_index.astype(jnp.float32))
        * trace_code.astype(jnp.float32)
        / LEVELS
    )
    block = hidden_all
    output = summed + lax.psum_scatter(
        jnp.dot(block, w_down, preferred_element_type=jnp.float32),
        "dp",
        scatter_dimension=0,
        tiled=True,
    )
    values = lax.psum(jnp.dot(output, critic_head, precision=highest), "ffn")
    value = jnp.sum(values * one_hot, axis=1)
    differ = value - targets
    picked = one_hot * (weight * differ)[:, None]
    out_grad = jnp.dot(picked, critic_head.T, precision=highest).astype(jnp.bfloat16)
    head_part = jnp.dot(output.T, picked, precision=highest)
    loss_part = 0.5 * jnp.sum(weight * differ * differ)
    grad_head, loss_sum = lax.psum((head_part, loss_part), "dp")
    loss = loss_sum / total_rows
    piece = lax.all_gather(out_grad, "dp", axis=0, tiled=True)
    block = hidden_all
    grad_acc = jnp.dot(block.T, piece, preferred_element_type=jnp.float32)
    update = jnp.dot(piece, w_down.T, preferred_element_type=jnp.float32)
    hidden_grad = lax.psum_scatter(update, "ffn", scatter_dimension=0, tiled=True)
    sigmoid_gate = jax.nn.sigmoid(gate)
    gate_grad = (hidden_grad * up_proj * sigmoid_gate * (1.0 + gate * (1.0 - sigmoid_gate))).astype(
        jnp.bfloat16
    )
    up_grad = (hidden_grad * jax.nn.silu(gate)).astype(jnp.bfloat16)
    paired_grads = jnp.concatenate([gate_grad, up_grad], axis=1)
    block = normed_all
    weight_grads = jnp.dot(
        block.T,
        lax.all_gather(paired_grads, "ffn", axis=0, tiled=True),
        preferred_element_type=jnp.float32,
    )
    grad_gate = weight_grads[:, :hidden_width]
    grad_up = weight_grads[:, hidden_width:]
    return (grad_gate, grad_up, grad_acc, grad_head, loss)


def solution(mesh):
    in_specs = (
        P("dp", "ffn"),
        P("dp", "ffn"),
        P("ffn"),
        P("ffn", "dp"),
        P("ffn", "dp"),
        P("dp", "ffn"),
        P("ffn", None),
        P("dp"),
        P("dp"),
        P("dp"),
        P("dp"),
    )
    out_specs = (P("ffn", "dp"), P("ffn", "dp"), P("dp", "ffn"), P("ffn", None), P())
    return jax.shard_map(body, mesh=mesh, in_specs=in_specs, out_specs=out_specs, check_vma=False)
```

profile of v0, /device:TPU:1, one launch (start us, length us, event | category | flops | bytes accessed | tf_op | source)
XLA Modules:
  0.0 557.2 jit_solution(15526293462578918214)
XLA Ops:
  7.2 0.0 copy-start
  7.2 0.0 all-gather.4.cloned.1.call-start
  7.2 1.1 multiply_reduce_fusion
  8.3 17.3 %psum.28 = f32[32]{0:T(128)S(1)} all-reduce(f32[32]{0:T(128)S(1)} %multiply_reduce_fusion), channel_id=1, replica_groups=mesh['dp'=32,'ffn'=8] {'ffn'}, use_global_device_ids=true, to_apply=%region_1.0 | all-reduce | flops 32 | bytes 256 | tf_op jit(solution)/shard_map/psum | solution.py:25
  25.6 1.6 multiply_convert_fusion.3
  27.2 0.0 all-gather.4.cloned.1.call-update
  27.2 0.0 reduce-scatter.4.cloned.1.call-start
  27.3 51.0 %all-gather.4.cloned.1.call-done = bf16[1024,1024]{1,0:T(8,128)(2,1)} async-done(((bf16[32,1024]{1,0:T(8,128)(2,1)}), bf16[1024,1024]{1,0:T(8,128)(2,1)}) %all-gather.4.cloned.1.call-update) | async-done | bytes 2097168 | tf_op jit(solution)/shard_map/all_gather | solution.py:27
  78.3 6.1 %fusion = f32[1024,924]{0,1:T(8,128)} fusion(bf16[1024,1024]{1,0:T(8,128)(2,1)} %all-gather.4.cloned.1.call-done, bf16[1024,462]{0,1:T(8,128)(2,1)} %param.15, bf16[1024,462]{0,1:T(8,128)(2,1)} %param.14), kind=kOutput, calls=%fused_computation | convolution fusion | flops 1941553152 | bytes 7774208 | tf_op jit(solution)/shard_map/dot_general | solution.py:33
  84.4 0.0 reduce-scatter.4.cloned.1.call-update
  84.4 0.0 reduce-scatter.6.cloned.1.call-start
  84.5 50.6 %reduce-scatter.4.cloned.1.call-done = f32[128,924]{0,1:T(8,128)} async-done(((f32[1024,924]{0,1:T(8,128)}), f32[128,924]{0,1:T(8,128)}) %reduce-scatter.4.cloned.1.call-update) | async-done | bytes 473104 | tf_op jit(solution)/shard_map/reduce_scatter | solution.py:32
  135.1 1.1 multiply_convert_fusion.2
  136.2 21.7 %all_gather.13 = bf16[1024,462]{0,1:T(8,128)(2,1)S(1)} all-gather(bf16[128,462]{0,1:T(8,128)(2,1)S(1)} %multiply_convert_fusion.2), channel_id=1, replica_groups=mesh['dp'=32,'ffn'=8] {'ffn'}, dimensions={0}, use_global_device_ids=true | all-gather | bytes 1064448 | tf_op jit(solution)/shard_map/all_gather | solution.py:41
  158.0 0.0 copy-done
  158.0 3.2 fusion.22
  161.2 0.0 copy-start.2
  161.2 0.0 copy-start.3
  161.2 0.0 copy-start.5
  161.2 0.0 copy-start.6
  161.2 0.0 copy-start.7
  161.2 0.0 copy-start.8
  161.2 0.0 copy-start.9
  161.3 0.0 reduce-scatter.6.cloned.1.call-update
  161.3 0.0 all-gather.6.cloned.1.call-start
  161.3 91.0 %reduce-scatter.6.cloned.1.call-done = f32[32,1024]{1,0:T(8,128)} async-done(((f32[1024,1024]{1,0:T(8,128)}), f32[32,1024]{1,0:T(8,128)}) %reduce-scatter.6.cloned.1.call-update) | async-done | bytes 131088 | tf_op jit(solution)/shard_map/reduce_scatter | solution.py:53
  252.3 0.0 copy-done.2
  252.3 0.0 copy-done.3
  252.3 0.0 copy-done.5
  252.3 1.1 fusion.8
  253.4 23.1 %psum.29 = f32[32,18]{0,1:T(8,128)S(1)} all-reduce(f32[32,18]{0,1:T(8,128)S(1)} %fusion.8), channel_id=1, replica_groups=mesh['dp'=32,'ffn'=8] {'ffn'}, use_global_device_ids=true, to_apply=%region_4.5 | all-reduce | flops 576 | bytes 4608 | tf_op jit(solution)/shard_map/psum | solution.py:59
  276.5 0.0 copy-done.6
  276.5 0.0 copy-done.7
  276.5 0.0 copy-done.8
  276.5 0.0 copy-done.9
  276.6 0.6 multiply_reduce_fusion.1
  277.2 0.9 convolution_convert_fusion
  278.1 0.0 all-gather.6.cloned.1.call-update
  278.1 0.0 reduce-scatter.8.cloned.1.call-start
  278.1 54.9 %all-gather.6.cloned.1.call-done = bf16[1024,1024]{1,0:T(8,128)(2,1)} async-done(((bf16[32,1024]{1,0:T(8,128)(2,1)}), bf16[1024,1024]{1,0:T(8,128)(2,1)}) %all-gather.6.cloned.1.call-update) | async-done | bytes 2097168 | tf_op jit(solution)/shard_map/all_gather | solution.py:68
  333.0 4.0 fusion.23
  337.0 0.0 copy-start.1
  337.0 0.0 copy-start.4
  337.0 0.0 reduce-scatter.8.cloned.1.call-update
  337.1 0.0 all-gather.8.cloned.1.call-start
  337.1 35.6 %reduce-scatter.8.cloned.1.call-done = f32[128,462]{0,1:T(8,128)} async-done(((f32[1024,462]{0,1:T(8,128)}), f32[128,462]{0,1:T(8,128)}) %reduce-scatter.8.cloned.1.call-update) | async-done | bytes 236560 | tf_op jit(solution)/shard_map/reduce_scatter | solution.py:72
  372.7 0.0 copy-done.1
  372.7 1.1 multiply_convert_fusion.1
  373.8 0.7 pad_maximum_fusion
  374.5 0.0 all-gather.8.cloned.1.call-update
  374.6 0.0 all-reduce.2.cloned.1.call-start
  375.3 68.3 %psum.31 = f32[]{:T(128)} all-reduce(f32[]{:T(128)S(6)} %mul_shard_map.3), channel_id=1, replica_groups=mesh['dp'=32,'ffn'=8] {'dp'}, use_global_device_ids=true, to_apply=%region_9.10 | all-reduce | flops 1 | bytes 8 | tf_op jit(solution)/shard_map/psum | solution.py:66
  444.2 0.0 copy-done.4
  444.2 0.9 fusion.6
  445.1 0.0 all-reduce.2.cloned.1.call-update
  445.1 4.0 fusion.25
  449.1 0.0 all-gather.8.cloned.1.call-done
  449.1 4.4 fusion.24
  453.5 2.3 fusion.21
  455.8 91.9 %all-reduce.2.cloned.1.call-done = f32[1024,18]{0,1:T(8,128)} async-done(((f32[1024,18]{0,1:T(8,128)}), f32[1024,18]{0,1:T(8,128)}) %all-reduce.2.cloned.1.call-update) | async-done | bytes 73744 | tf_op jit(solution)/shard_map/psum | solution.py:66
  547.7 1.5 copy.17
  (2 shorter events, 0.0 us)
Async XLA Ops:
  7.2 150.8 %copy-start = (bf16[462,1024]{1,0:T(8,128)(2,1)S(1)}, bf16[462,1024]{1,0:T(8,128)(2,1)}, u32[]{:S(2)}) copy-start(bf16[462,1024]{1,0:T(8,128)(2,1)} %param.16) | copy-start | bytes 2838532
  7.2 71.1 %all-gather.4.cloned.1.call-start = ((), (), s32[]{:S(2)}) async-start(), calls=%async_computation.3 | async-start | bytes 2162688 | tf_op jit(solution)/shard_map/all_gather | solution.py:27
  27.2 107.9 %reduce-scatter.4.cloned.1.call-start = ((), (), s32[]{:S(2)}) async-start(), calls=%async_computation.4 | async-start | bytes 4276224 | tf_op jit(solution)/shard_map/reduce_scatter | solution.py:32
  84.4 167.9 %reduce-scatter.6.cloned.1.call-start = ((), (), s32[]{:S(2)}) async-start(), calls=%async_computation.5 | async-start | bytes 4325376 | tf_op jit(solution)/shard_map/reduce_scatter | solution.py:53
  161.2 91.1 %copy-start.2 = (bf16[32,1024]{1,0:T(8,128)(2,1)S(1)}, bf16[32,1024]{1,0:T(8,128)(2,1)}, u32[]{:S(2)}) copy-start(bf16[32,1024]{1,0:T(8,128)(2,1)} %param.12) | copy-start | bytes 196612
  161.2 91.1 %copy-start.3 = (bf16[32,1024]{1,0:T(8,128)(2,1)S(1)}, bf16[32,1024]{1,0:T(8,128)(2,1)}, u32[]{:S(2)}) copy-start(bf16[32,1024]{1,0:T(8,128)(2,1)} %param.11) | copy-start | bytes 196612
  161.2 91.1 %copy-start.5 = (bf16[1024,18]{0,1:T(8,128)(2,1)S(1)}, bf16[1024,18]{0,1:T(8,128)(2,1)}, u32[]{:S(2)}) copy-start(bf16[1024,18]{0,1:T(8,128)(2,1)} %param.17) | copy-start | bytes 110596
  161.2 115.3 %copy-start.6 = (s32[32]{0:T(128)S(1)}, s32[32]{0:T(128)}, u32[]{:S(2)}) copy-start(s32[32]{0:T(128)} %param.18) | copy-start | bytes 388
  161.2 115.3 %copy-start.7 = (s32[32]{0:T(128)S(1)}, s32[32]{0:T(128)}, u32[]{:S(2)}) copy-start(s32[32]{0:T(128)} %param.20) | copy-start | bytes 388
  161.2 115.3 %copy-start.8 = (s32[32]{0:T(128)S(1)}, s32[32]{0:T(128)}, u32[]{:S(2)}) copy-start(s32[32]{0:T(128)} %param.19) | copy-start | bytes 388
  161.2 115.3 %copy-start.9 = (f32[32]{0:T(128)S(1)}, f32[32]{0:T(128)}, u32[]{:S(2)}) copy-start(f32[32]{0:T(128)} %param.21) | copy-start | bytes 388
  161.3 171.7 %all-gather.6.cloned.1.call-start = ((), (), s32[]{:S(2)}) async-start(), calls=%async_computation.6 | async-start | bytes 2162688 | tf_op jit(solution)/shard_map/all_gather | solution.py:68
  278.1 94.6 %reduce-scatter.8.cloned.1.call-start = ((), (), s32[]{:S(2)}) async-start(), calls=%async_computation.7 | async-start | bytes 2138112 | tf_op jit(solution)/shard_map/reduce_scatter | solution.py:72
  337.0 35.7 %copy-start.1 = (f32[128,924]{0,1:T(8,128)S(1)}, f32[128,924]{0,1:T(8,128)}, u32[]{:S(2)}) copy-start(f32[128,924]{0,1:T(8,128)} %reduce-scatter.4.cloned.1.call-done) | copy-start | bytes 1419268
  337.0 107.1 %copy-start.4 = (f32[32,1024]{1,0:T(8,128)S(1)}, f32[32,1024]{1,0:T(8,128)}, u32[]{:S(2)}) copy-start(f32[32,1024]{1,0:T(8,128)} %reduce-scatter.6.cloned.1.call-done) | copy-start | bytes 393220
  337.1 112.0 %all-gather.8.cloned.1.call-start = ((), (), s32[]{:S(2)}) async-start(), calls=%async_computation.8 | async-start | bytes 2138112 | tf_op jit(solution)/shard_map/all_gather | solution.py:82
  374.6 173.1 %all-reduce.2.cloned.1.call-start = ((), (), s32[]{:S(2)}) async-start(), calls=%async_computation.9 | async-start | bytes 196608 | tf_op jit(solution)/shard_map/psum | solution.py:66
Sparse Core Ops, SparseCore 0:
  27.3 50.9 all-gather.3
  84.6 50.4 reduce-scatter.3
  161.4 90.8 reduce-scatter.5
  278.2 54.7 all-gather.5
  337.2 35.4 reduce-scatter.7
  375.0 45.5 all-gather.7
  445.2 102.3 all-reduce.1
where the time goes:
time: 558 us; the launch traced here: 557 us
  waiting for transfers between devices  375 us (67%)
  blocking collectives  130 us (23%)
  matrix products  24.6 us (4%)
  between operations  16.6 us (3%)
  other arithmetic  6.26 us (1%)
    psum x1, waiting for transfers between devices, body(): grad_head, loss_sum = lax.psum((head_part, loss_part), 'dp')  91.9 us
    reduce_scatter x1, waiting for transfers between devices, body(): lax.psum_scatter(jnp.dot(block, w_down, preferred_element_type=jnp.float3...  91 us
    psum x1, blocking collectives, body(): grad_head, loss_sum = lax.psum((head_part, loss_part), 'dp')  68.3 us
    all_gather x1, waiting for transfers between devices, body(): piece = lax.all_gather(out_grad, 'dp', axis=0, tiled=True)  54.9 us
    all_gather x1, waiting for transfers between devices, body(): normed_all = lax.all_gather(normed, 'dp', axis=0, tiled=True)  51 us
    reduce_scatter x1, waiting for transfers between devices, body(): lax.psum_scatter(jnp.dot(block, paired, preferred_element_type=jnp.float3...  50.6 us
    reduce_scatter x1, waiting for transfers between devices, body(): lax.psum_scatter(update, 'ffn', scatter_dimension=0, tiled=True)  35.6 us
    psum x1, blocking collectives, body(): values = lax.psum(jnp.dot(output, critic_head, precision=highest), 'ffn')  23.1 us
  transfers between devices with their start and end apart: 7, of which 6 were waited for; matrix products, arithmetic and copies ran while one was open for 2% of the time, Pallas kernels for 0%

commit v1 on v0

v1 whole, which is shorter than its diff:
```python
import functools

import jax
import jax.numpy as jnp
from jax import lax
from jax.experimental import pallas as pl
from jax.experimental.pallas import tpu as pltpu
from jax.sharding import PartitionSpec as P

MESH = pl.DeviceIdType.MESH
F32 = jnp.float32
BF16 = jnp.bfloat16
LEVELS = 8
ROWS = 32
NT = (((1,), (1,)), ((), ()))
NN = (((1,), (0,)), ((), ()))


def dot(a, b, dims=NN):
    return lax.dot_general(a, b, dims, preferred_element_type=F32)


def two(a):
    high = a.astype(BF16)
    return high, (a - high.astype(F32)).astype(BF16)


def exchange_kernel(
    nx,
    ny,
    nz,
    resid_ref,
    attn_ref,
    gain_ref,
    w_gate_hbm,
    w_up_hbm,
    w_down_hbm,
    w_head_ref,
    info_ref,
    xct_hbm,
    q_hbm,
    h_ref,
    head_ref,
    loss_ref,
    wheadt_ref,
    w_gate,
    w_up,
    w_down,
    wt,
    x_all,
    xt,
    zsum,
    meta,
    gpart,
    grecv,
    gfull,
    hpart,
    hrecv,
    hfull,
    psum,
    rs_send,
    rs_recv,
    q_all,
    vsum,
    zcoef,
    hd_core,
    hd_x,
    hd_y,
    send_sem,
    recv_sem,
    local_sem,
):
    i = lax.axis_index("dp")
    z = lax.axis_index("ffn")
    core = i % 2
    y = (i // 2) % ny
    x = i // (2 * ny)
    own, depth = resid_ref.shape
    hidden = w_down.shape[0]
    fp = wt.shape[1]
    half = nz // 2
    tokens = own * nx * ny * 2
    chunk = tokens // nz
    rep = chunk // own
    acts = w_head_ref.shape[1]

    def at_x(k):
        return (((x + k) % nx * ny + y) * 2 + core, z)

    def at_y(k):
        return ((x * ny + (y + k) % ny) * 2 + core, z)

    def at_z(k):
        return (i, (z + k) % nz)

    sibling = ((x * ny + y) * 2 + 1 - core, z)

    next_sem = [0]
    sends = []

    def copy_pair(src, dst, landing, device):
        n = next_sem[0]
        next_sem[0] += 1
        out = pltpu.make_async_remote_copy(
            src_ref=src,
            dst_ref=dst,
            send_sem=send_sem.at[n],
            recv_sem=recv_sem.at[n],
            device_id=device,
            device_id_type=MESH,
        )
        into = pltpu.make_async_remote_copy(
            src_ref=landing,
            dst_ref=landing,
            send_sem=send_sem.at[n],
            recv_sem=recv_sem.at[n],
            device_id=device,
            device_id_type=MESH,
        )
        sends.append(out)
        return out, into

    def spread(slots, me, n, at):
        arrivals = []
        for k in range(1, n):
            out, into = copy_pair(slots.at[me], slots.at[me], slots.at[(me + n - k) % n], at(k))
            out.start()
            arrivals.append(into)
        return arrivals

    def land(arrivals):
        for into in arrivals:
            into.wait_recv()

    at_core = lambda k: sibling

    def total(slots, n):
        result = slots[0]
        for k in range(1, n):
            result = result + slots[k]
        return result

    peers = [at_x(k) for k in range(1, nx)] + [at_y(k) for k in range(1, ny)]
    peers += [at_z(k) for k in range(1, nz)] + [sibling]
    barrier = pltpu.get_barrier_semaphore()
    for peer in peers:
        pl.semaphore_signal(barrier, inc=1, device_id=peer, device_id_type=MESH)

    loads = []
    for n, (src, dst) in enumerate(((w_gate_hbm, w_gate), (w_up_hbm, w_up), (w_down_hbm, w_down))):
        load = pltpu.make_async_copy(src, dst, local_sem.at[n])
        load.start()
        loads.append(load)

    row = lax.broadcasted_iota(jnp.int32, (own, chunk), 0)
    lane = lax.broadcasted_iota(jnp.int32, (own, chunk), 1)
    row8 = lax.broadcasted_iota(jnp.int32, (8, chunk), 0)
    lane8 = lax.broadcasted_iota(jnp.int32, (8, chunk), 1)
    action_row = lax.broadcasted_iota(jnp.int32, (ROWS, chunk), 0).astype(F32)

    def lanes_of(column):
        return jnp.sum(jnp.where(lane % own == row, column, 0.0), axis=0, keepdims=True)

    def rows_of(vector):
        return jnp.sum(jnp.where(lane == row, vector, 0.0), axis=1, keepdims=True)

    def stack(*vectors):
        block = jnp.zeros((8, chunk), F32)
        for n, vector in enumerate(vectors):
            block = jnp.where(row8 == n, vector, block)
        return block

    summed = resid_ref[...].astype(F32) + attn_ref[...].astype(F32)
    squares = jnp.sum(summed * summed, axis=1, keepdims=True)
    w_head = w_head_ref[...]
    action_own = info_ref[:, 2:3]
    one_hot_own = lax.broadcasted_iota(jnp.int32, (own, acts), 1).astype(F32) == action_own
    scores = dot(resid_ref[...], w_head) + dot(attn_ref[...], w_head)
    score = jnp.sum(jnp.where(one_hot_own, scores, 0.0), axis=1, keepdims=True)
    zsum[z] = stack(lanes_of(squares), lanes_of(score))

    pl.semaphore_wait(barrier, len(peers))
    zsum_in = spread(zsum, z, nz, at_z)

    eye = (
        lax.broadcasted_iota(jnp.int32, (fp, hidden), 0)
        == lax.broadcasted_iota(jnp.int32, (fp, hidden), 1)
    ).astype(BF16)
    loads[0].wait()
    wt[0] = dot(eye, w_gate[...], NT).astype(BF16)
    loads[1].wait()
    wt[1] = dot(eye, w_up[...], NT).astype(BF16)

    land(zsum_in)
    zboth = total(zsum, nz)
    mean = rows_of(zboth[0:1]) / (depth * nz)
    normed = (summed * lax.rsqrt(mean + 1e-06) * gain_ref[...]).astype(BF16)
    hr = own // 2
    x_all[x, y, core, 0] = normed[:hr]
    x_all[x, y, core, 1] = normed[hr:]

    first_a, first_b = [], []
    for k in range(1, nx):
        mine = x_all.at[x, y, core, 0]
        out, into = copy_pair(mine, mine, x_all.at[(x + nx - k) % nx, y, core, 0], at_x(k))
        out.start()
        first_a.append(into)
    for k in range(1, ny):
        mine = x_all.at[x, y, core, 1]
        out, into = copy_pair(mine, mine, x_all.at[x, (y + ny - k) % ny, core, 1], at_y(k))
        out.start()
        first_b.append(into)

    base = lanes_of(info_ref[:, 0:1])
    mine8 = (lane8 // own == i % rep) & (jnp.full((8, chunk), i // rep, jnp.int32) == z)
    block = stack(
        zboth[1:2] - lanes_of(info_ref[:, 1:2]), base, lanes_of(action_own)
    )
    meta[0, core] = jnp.where(mine8, block, 0.0)
    meta_in = spread(meta.at[0], core, 2, at_core)

    eye_acts = (
        lax.broadcasted_iota(jnp.int32, (ROWS, acts), 0)
        == lax.broadcasted_iota(jnp.int32, (ROWS, acts), 1)
    ).astype(BF16)
    w_head_t = dot(eye_acts, w_head, NT).astype(BF16)
    wheadt_ref[...] = w_head_t

    cuts = nz // 4
    width = gpart.shape[2]

    def put_pieces(pieces, value):
        for p in range(nz):
            r, c = p // cuts, p % cuts
            pieces[p] = value[8 * r : 8 * r + 8, c * width : (c + 1) * width]

    def reduce_start(part, recv):
        arrivals = []
        for k in range(1, nz):
            out, into = copy_pair(
                part.at[(z + k) % nz], recv.at[z], recv.at[(z + nz - k) % nz], at_z(k)
            )
            out.start()
            arrivals.append(into)
        return arrivals

    def reduce_middle(arrivals, part, recv, full):
        recv[z] = part[z]
        land(arrivals)
        full[z] = total(recv, nz)
        return spread(full, z, nz, at_z)

    def pieces_of(full):
        rows = [
            jnp.concatenate([full[r * cuts + c] for c in range(cuts)], axis=1) for r in range(4)
        ]
        return jnp.concatenate(rows, axis=0)

    def wide(value):
        return jnp.concatenate(
            [value, jnp.zeros((ROWS, cuts * width - value.shape[1]), F32)], axis=1
        )

    loads[2].wait()
    put_pieces(gpart, wide(dot(w_head_t, w_down[...], NT)))
    g_in = reduce_start(gpart, grecv)

    land(first_a)
    second_a, second_b, third = [], [], []

    def pass_a(k):
        other = (y + ny - k) % ny
        part = x_all.at[:, other, core, 0]
        out, into = copy_pair(part, part, x_all.at[:, other, 1 - core, 0], sibling)
        out.start()
        third.append(into)

    def pass_b(k):
        other = (x + nx - k) % nx
        part = x_all.at[other, :, core, 1]
        out, into = copy_pair(part, part, x_all.at[other, :, 1 - core, 1], sibling)
        out.start()
        third.append(into)

    for k in range(1, ny):
        part = x_all.at[:, y, core, 0]
        out, into = copy_pair(part, part, x_all.at[:, (y + ny - k) % ny, core, 0], at_y(k))
        out.start()
        second_a.append(into)
    land(first_b)
    for k in range(1, nx):
        part = x_all.at[x, :, core, 1]
        out, into = copy_pair(part, part, x_all.at[(x + nx - k) % nx, :, core, 1], at_x(k))
        out.start()
        second_b.append(into)
    pass_a(0)
    pass_b(0)

    land(meta_in)
    meta[1, x] = meta[0, 0] + meta[0, 1]
    meta_in = spread(meta.at[1], x, nx, at_x)
    g_in = reduce_middle(g_in, gpart, grecv, gfull)

    for k in range(1, max(nx, ny)):
        if k < ny:
            second_a[k - 1].wait_recv()
            pass_a(k)
        if k < nx:
            second_b[k - 1].wait_recv()
            pass_b(k)
    land(meta_in)
    meta[2, y] = total(meta.at[1], nx)
    meta_in = spread(meta.at[2], y, ny, at_y)
    land(third)

    chips = rep // 2

    def tokens_of(c):
        rows = x_all[c * chips // ny, pl.ds(c * chips % ny, chips)]
        return rows.reshape(chunk, depth)

    hops = {(d, h): half if d == h else half - 1 for d in (0, 1) for h in (0, 1)}
    order = ((0, 0), (1, 1), (0, 1), (1, 0))
    sign = (1, -1)

    def chunk_at(offset):
        return (z + nz + offset) % nz

    waiting = {}
    for o in range(half, 0, -1):
        chosen = [dh for dh in order if hops[dh] >= o]
        for d in (0, 1):
            block = tokens_of(chunk_at(sign[d] * o))
            for h in (0, 1):
                if (d, h) in chosen:
                    psum[d, h] = dot(wt[h], block, NT)
        for d, h in chosen:
            s = hops[d, h] - o
            value = psum[d, h]
            if s > 0:
                waiting[d, h].wait_recv()
                value = value + rs_recv[d, h, s - 1].astype(F32)
            rs_send[d, h, s] = value.astype(BF16)
            out, into = copy_pair(
                rs_send.at[d, h, s], rs_recv.at[d, h, s], rs_recv.at[d, h, s], at_z(sign[d] % nz)
            )
            out.start()
            waiting[d, h] = into

    block = tokens_of(z)
    for h in (0, 1):
        psum[0, h] = dot(wt[h], block, NT)
    land(meta_in)
    info = total(meta.at[2], ny)
    land(g_in)
    g_full = jnp.transpose(pieces_of(gfull))[:fp]
    one_hot = (action_row == info[2:3]).astype(BF16)
    g_high, g_low = two(g_full)
    picked_g = dot(g_high, one_hot) + dot(g_low, one_hot)

    def all_sum(h):
        value = psum[0, h]
        for d in (h, 1 - h):
            waiting[d, h].wait_recv()
            value = value + rs_recv[d, h, hops[d, h] - 1].astype(F32)
        return value

    gate = all_sum(0)
    up = all_sum(1)
    sg = 1.0 / (1.0 + jnp.exp(-gate))
    silu = gate * sg
    lanes = pl.ds(pl.multiple_of(z * chunk, chunk), chunk)
    q_all[0, :, lanes] = (picked_g * up * sg * (1.0 + gate * (1.0 - sg))).astype(BF16)
    q_all[1, :, lanes] = (picked_g * silu).astype(BF16)

    arriving = {}

    def pass_q(d, h, s):
        def piece(c):
            return q_all.at[h, :, pl.ds(pl.multiple_of(c * chunk, chunk), chunk)]

        if s > 0:
            arriving[d, h].wait_recv()
        mine = piece(chunk_at(-sign[d] * s))
        out, into = copy_pair(
            mine, mine, piece(chunk_at(-sign[d] * (s + 1))), at_z(sign[d] % nz)
        )
        out.start()
        arriving[d, h] = into

    for d, h in order:
        pass_q(d, h, 0)

    act = (silu * up).astype(BF16).astype(F32)
    v = jnp.sum(act * picked_g, axis=0, keepdims=True)
    vsum[0, core] = stack(v)
    land(spread(vsum.at[0], core, 2, at_core))
    vsum[1, x] = vsum[0, 0] + vsum[0, 1]
    land(spread(vsum.at[1], x, nx, at_x))
    vsum[2, y] = total(vsum.at[1], nx)
    land(spread(vsum.at[2], y, ny, at_y))
    v_all = total(vsum.at[2], ny)
    differ = info[0:1] + v_all[0:1]
    weight = info[1:2]
    coef = weight * differ
    zcoef[z] = stack(coef, info[2:3], weight * differ * differ)
    zcoef_in = spread(zcoef, z, nz, at_z)

    act_high, act_low = two(act * coef)
    put_pieces(hpart, wide(dot(one_hot, act_high, NT) + dot(one_hot, act_low, NT)))
    h_in = reduce_start(hpart, hrecv)

    for d, h in order:
        if hops[d, h] > 1:
            pass_q(d, h, 1)

    land(zcoef_in)
    h_in = reduce_middle(h_in, hpart, hrecv, hfull)

    loss_rows = total(zcoef, nz)[2:3]
    loss = 0.5 * jnp.sum(loss_rows, axis=1, keepdims=True) / tokens
    loss_ref[...] = jnp.broadcast_to(loss, (8, chunk))

    out_copies = []
    for c in range(nz):
        block = jnp.transpose(tokens_of(c)).astype(F32)
        xt[:, c * chunk : (c + 1) * chunk] = (block * zcoef[c, 0:1]).astype(BF16)
    out = pltpu.make_async_copy(xt, xct_hbm, local_sem.at[3])
    out.start()
    out_copies.append(out)

    land(h_in)
    h_sum = pieces_of(hfull)
    h_ref[...] = jnp.transpose(h_sum)

    h_high, h_low = two(h_sum[:, :hidden])
    head = dot(h_high, w_down[...]) + dot(h_low, w_down[...])
    own_block = zcoef[i // rep]
    lane32 = lax.broadcasted_iota(jnp.int32, (ROWS, chunk), 1)
    picked = jnp.where(
        (action_row == own_block[1:2]) & (lane32 // own == i % rep), own_block[0:1], 0.0
    )
    p_high, p_low = two(picked)
    for ref in (resid_ref, attn_ref):
        rows = jnp.concatenate([ref[...]] * rep, axis=0)
        head = head + dot(p_high, rows) + dot(p_low, rows)
    wide_half = depth // 2
    for c in (0, 1):
        hd_core[c] = head[: hd_core.shape[1], c * wide_half : (c + 1) * wide_half]
    out, into = copy_pair(hd_core.at[1 - core], hd_core.at[2], hd_core.at[2], sibling)
    out.start()

    for s in range(2, half):
        if s == 2:
            into.wait_recv()
            hd_x[x] = hd_core[core] + hd_core[2]
            hd_in = spread(hd_x, x, nx, at_x)
        for d, h in order:
            if hops[d, h] > s:
                pass_q(d, h, s)
        if s == 2:
            land(hd_in)
            hd_y[y] = total(hd_x, nx)
            hd_in = spread(hd_y, y, ny, at_y)
    if half <= 2:
        into.wait_recv()
        hd_x[x] = hd_core[core] + hd_core[2]
        land(spread(hd_x, x, nx, at_x))
        hd_y[y] = total(hd_x, nx)
        hd_in = spread(hd_y, y, ny, at_y)
    land(hd_in)
    hd_core[3 + core] = total(hd_y, ny)
    out, into = copy_pair(
        hd_core.at[3 + core], hd_core.at[3 + core], hd_core.at[4 - core], sibling
    )
    out.start()
    into.wait_recv()
    head_ref[...] = jnp.concatenate([hd_core[3], hd_core[4]], axis=1)

    for d, h in order:
        arriving[d, h].wait_recv()
    out = pltpu.make_async_copy(q_all, q_hbm, local_sem.at[4])
    out.start()
    out_copies.append(out)
    for out in sends:
        out.wait_send()
    for out in out_copies:
        out.wait()


def grads_kernel(xct_ref, q_ref, h_ref, head_ref, loss_ref, wheadt_ref, gg, gu, gd, gh, loss):
    hidden, acts = gd.shape[0], gh.shape[1]
    fp = q_ref.shape[1]
    block = xct_ref[...]
    gg[...] = dot(block, q_ref[0], NT)[:, :hidden]
    gu[...] = dot(block, q_ref[1], NT)[:, :hidden]
    h_high, h_low = two(h_ref[:fp])
    head_t = wheadt_ref[...]
    gd[...] = (dot(h_high, head_t) + dot(h_low, head_t))[:hidden]
    gh[...] = jnp.transpose(head_ref[...])[:, :acts]
    loss[0, 0] = loss_ref[0, 0]


def body(
    nx,
    ny,
    nz,
    resid,
    attn_out,
    norm_gain,
    w_gate,
    w_up,
    w_down,
    w_head,
    actions,
    step_index,
    trace_code,
    targets,
):
    own, depth = resid.shape
    hidden = w_down.shape[0]
    acts = w_head.shape[1]
    fp = -(-hidden // 16) * 16
    fl = -(-hidden // 128) * 128
    tokens = own * nx * ny * 2
    chunk = tokens // nz
    half = nz // 2
    cuts = nz // 4
    head_rows = -(-acts // 8) * 8
    weight = (
        jnp.power(jnp.float32(0.97), step_index.astype(F32)) * trace_code.astype(F32) / LEVELS
    )
    info = jnp.stack([weight, targets, actions.astype(F32)], axis=1)
    info = jnp.pad(info, ((0, 0), (0, 125)))
    vmem = pl.BlockSpec(memory_space=pltpu.VMEM)
    anywhere = pl.BlockSpec(memory_space=pl.ANY)
    shape = jax.ShapeDtypeStruct
    n_sems = (
        2 * (nx - 1 + ny - 1) + nx + ny + 3 * (1 + nx - 1 + ny - 1) + 1 + 6 * (nz - 1)
        + 2 * 2 * (2 * half - 1)
    )
    pieces = pltpu.VMEM((nz, 8, fl // cuts), F32)
    xct, q, h, head, loss, w_head_t = pl.pallas_call(
        functools.partial(exchange_kernel, nx, ny, nz),
        out_shape=(
            shape((depth, tokens), BF16),
            shape((2, fp, tokens), BF16),
            shape((fl, ROWS), F32),
            shape((head_rows, depth), F32),
            shape((8, chunk), F32),
            shape((ROWS, depth), BF16),
        ),
        in_specs=[vmem, vmem, vmem, anywhere, anywhere, anywhere, vmem, vmem],
        out_specs=(anywhere, anywhere, vmem, vmem, vmem, vmem),
        scratch_shapes=[
            pltpu.VMEM(w_gate.shape, BF16),
            pltpu.VMEM(w_up.shape, BF16),
            pltpu.VMEM(w_down.shape, BF16),
            pltpu.VMEM((2, fp, depth), BF16),
            pltpu.VMEM((nx, ny, 2, 2, own // 2, depth), BF16),
            pltpu.VMEM((depth, tokens), BF16),
            pltpu.VMEM((nz, 8, chunk), F32),
            pltpu.VMEM((3, max(nx, ny), 8, chunk), F32),
            pieces,
            pieces,
            pieces,
            pieces,
            pieces,
            pieces,
            pltpu.VMEM((2, 2, fp, chunk), F32),
            pltpu.VMEM((2, 2, half, fp, chunk), BF16),
            pltpu.VMEM((2, 2, half, fp, chunk), BF16),
            pltpu.VMEM((2, fp, tokens), BF16),
            pltpu.VMEM((3, max(nx, ny), 8, chunk), F32),
            pltpu.VMEM((nz, 8, chunk), F32),
            pltpu.VMEM((5, head_rows, depth // 2), F32),
            pltpu.VMEM((nx, head_rows, depth // 2), F32),
            pltpu.VMEM((ny, head_rows, depth // 2), F32),
            pltpu.SemaphoreType.DMA((n_sems,)),
            pltpu.SemaphoreType.DMA((n_sems,)),
            pltpu.SemaphoreType.DMA((5,)),
        ],
        compiler_params=pltpu.CompilerParams(
            collective_id=0, has_side_effects=True, vmem_limit_bytes=40 * 1024 * 1024
        ),
        name="exchange",
    )(resid, attn_out, norm_gain.reshape(1, depth), w_gate, w_up, w_down, w_head, info)

    tile = min(256, depth)
    grad_gate, grad_up, grad_down, grad_head, loss = pl.pallas_call(
        grads_kernel,
        grid=(depth // tile,),
        out_shape=(
            shape((depth, hidden), F32),
            shape((depth, hidden), F32),
            shape((hidden, depth), F32),
            shape((depth, acts), F32),
            shape((1, 1), F32),
        ),
        in_specs=[
            pl.BlockSpec((tile, tokens), lambda n: (n, 0)),
            pl.BlockSpec((2, fp, tokens), lambda n: (0, 0, 0)),
            pl.BlockSpec((fl, ROWS), lambda n: (0, 0)),
            pl.BlockSpec((head_rows, tile), lambda n: (0, n)),
            pl.BlockSpec((8, chunk), lambda n: (0, 0)),
            pl.BlockSpec((ROWS, tile), lambda n: (0, n)),
        ],
        out_specs=(
            pl.BlockSpec((tile, hidden), lambda n: (n, 0)),
            pl.BlockSpec((tile, hidden), lambda n: (n, 0)),
            pl.BlockSpec((hidden, tile), lambda n: (0, n)),
            pl.BlockSpec((tile, acts), lambda n: (n, 0)),
            pl.BlockSpec((1, 1), lambda n: (0, 0), memory_space=pltpu.SMEM),
        ),
        compiler_params=pltpu.CompilerParams(vmem_limit_bytes=40 * 1024 * 1024),
        name="weight_grads",
    )(xct, q, h, head, loss, w_head_t)
    return grad_gate, grad_up, grad_down, grad_head, loss.reshape(())


def build(mesh, nx, ny):
    nz = mesh.shape["ffn"]
    in_specs = (
        P("dp", "ffn"),
        P("dp", "ffn"),
        P("ffn"),
        P("ffn", "dp"),
        P("ffn", "dp"),
        P("dp", "ffn"),
        P("ffn", None),
        P("dp"),
        P("dp"),
        P("dp"),
        P("dp"),
    )
    out_specs = (P("ffn", "dp"), P("ffn", "dp"), P("dp", "ffn"), P("ffn", None), P())
    return jax.shard_map(
        functools.partial(body, nx, ny, nz),
        mesh=mesh,
        in_specs=in_specs,
        out_specs=out_specs,
        check_vma=False,
    )


def solution(mesh):
    return build(mesh, 4, 4)
```

time: 558 us -> 101 us (0.18)
  waiting for transfers between devices: 375 us -> 0 us
  blocking collectives: 130 us -> 0 us
  Pallas kernels: 0 us -> 86.9 us
  matrix products: 24.6 us -> 0 us
  between operations: 16.6 us -> 0.73 us
  local copies, waits for them, and re-layouts: 3.92 us -> 10.9 us
    reduce_scatter x3 -> x0, waiting for transfers between devices: 177 us -> none  [the longest x1 91 us: body(): lax.psum_scatter(jnp.dot(block, w_down, preferred_element_type=jnp.float3...]
    psum x3 -> x0, blocking collectives: 109 us -> none  [the longest x1 68.3 us: body(): grad_head, loss_sum = lax.psum((head_part, loss_part), 'dp')]
    all_gather x3 -> x0, waiting for transfers between devices: 106 us -> none  [the longest x1 54.9 us: body(): piece = lax.all_gather(out_grad, 'dp', axis=0, tiled=True)]
    psum x1 -> x0, waiting for transfers between devices: 91.9 us -> none  [body(): grad_head, loss_sum = lax.psum((head_part, loss_part), 'dp')]
    pallas_call x0 -> x2, Pallas kernels: none -> 86.9 us  [the longest x1 82.6 us: body(): pl.pallas_call(functools.partial(exchange_kernel, nx, ny, nz), out_shape=...]
    dot_general x8 -> x0, matrix products: 24.6 us -> none  [the longest x1 6.1 us: body(): jnp.dot(block, paired, preferred_element_type=jnp.float32)]
    all_gather x1 -> x0, blocking collectives: 21.7 us -> none  [body(): hidden_all = lax.all_gather(hidden, 'ffn', axis=0, tiled=True)]
    unnamed x21 -> x16, local copies, waits for them, and re-layouts: 1.59 us -> 10.8 us
  transfers between devices with their start and end apart: 7 -> 0, of which waited for: 6 -> 0; matrix products, arithmetic and copies ran while one was open for 2% -> 0% of each run, Pallas kernels for 0% -> 0%
where the time goes in v1:
time: 101 us
  Pallas kernels  86.9 us (86%)
  local copies, waits for them, and re-layouts  10.9 us (11%)
  other arithmetic  2.01 us (2%)
    pallas_call x1, Pallas kernels, body(): pl.pallas_call(functools.partial(exchange_kernel, nx, ny, nz), out_shape=...  82.6 us
    unnamed x16, local copies, waits for them, and re-layouts  10.8 us
    pallas_call x1, Pallas kernels, body(): pl.pallas_call(grads_kernel, grid=(depth // tile,), out_shape=(shape((dep...  4.37 us

profile of v1, /device:TPU:1, one launch (start us, length us, event | category | flops | bytes accessed | tf_op | source)
XLA Modules:
  0.0 100.5 jit_solution(2413960977086142120)
XLA Ops:
  0.6 0.7 convert_bitcast_fusion
  1.3 0.7 multiply_bitcast_fusion
  2.0 0.7 pad_maximum_fusion
  2.6 0.1 copy.25
  2.7 1.0 copy.28.w_head_ref
  3.7 0.0 copy-start.1
  3.7 0.0 copy-start.2
  3.7 0.0 copy-start.3
  3.8 0.0 copy-start.4
  3.8 1.6 %copy.26.w_gate_hbm = bf16[1024,462]{1,0:T(8,128)(2,1)S(1)} copy(bf16[1024,462]{0,1:T(8,128)(2,1)} %param.14) | data formatting | bytes 1892352 | tf_op args[3]
  5.3 1.5 %copy.27.w_up_hbm = bf16[1024,462]{1,0:T(8,128)(2,1)S(1)} copy(bf16[1024,462]{0,1:T(8,128)(2,1)} %param.15) | data formatting | bytes 1892352 | tf_op args[4]
  6.8 0.0 copy-done.1
  6.8 0.0 copy-done.2
  6.8 0.0 copy-done.3
  6.8 0.0 copy-done.4
  6.9 82.6 %exchange.1 = (bf16[1024,1024]{1,0:T(8,128)(2,1)S(1)}, bf16[2,464,1024]{2,1,0:T(8,128)(2,1)S(1)}, f32[512,32]{1,0:T(8,128)S(1)}, f32[24,1024]{1,0:T(8,128)S(1)},...) custom-call(bf16[32,1024]{1,0:T(8,128)(2,1)S(1)} %copy-done.2, bf16[32,1024]{1,0:T(8,128)(2,1)S(1)} %copy-done.3, ...), custom_call_target="tpu_custom_call" | custom-call | tf_op jit(solution)/shard_map/exchange/pallas_call | solution.py:543
  89.4 4.4 %weight_grads.1 = (f32[1024,462]{1,0:T(8,128)S(1)}, f32[1024,462]{1,0:T(8,128)S(1)}, f32[462,1024]{1,0:T(8,128)}, f32[1024,18]{1,0:T(8,128)S(1)}, f32[1,1]{1,0:T(1,128)}) custom-call(bf16[1024,1024]{1,0:T(8,128)(2,1)S(1)} %get-tuple-element.16.xct_ref, bf16[2,464,1024]{2,1,0:T(8,128)(2,1)S(1)} %get-tuple-element.17.q_ref, ...), custom_call_target="tpu_custom_call" | custom-call | tf_op jit(solution)/shard_map/weight_grads/pallas_call | solution.py:590
  93.8 0.0 copy-start
  93.8 1.4 %copy-done = f32[1024,462]{1,0:T(8,128)} copy-done((f32[1024,462]{1,0:T(8,128)}, f32[1024,462]{1,0:T(8,128)S(1)}, u32[]{:S(2)}) %copy-start) | copy-done | bytes 1892376
  95.2 2.8 %copy.29 = f32[1024,462]{0,1:T(8,128)} copy(f32[1024,462]{1,0:T(8,128)} %copy-done) | data formatting | bytes 3784704
  98.0 0.8 copy.31
  98.8 1.7 %copy.30 = f32[1024,462]{0,1:T(8,128)} copy(f32[1024,462]{1,0:T(8,128)S(1)} %get-tuple-element.33) | data formatting | bytes 3784704
  (1 shorter events, 0.0 us)
Async XLA Ops:
  3.7 3.1 %copy-start.1 = (bf16[462,1024]{1,0:T(8,128)(2,1)S(1)}, bf16[462,1024]{1,0:T(8,128)(2,1)}, u32[]{:S(2)}) copy-start(bf16[462,1024]{1,0:T(8,128)(2,1)} %w_down_hbm.1) | copy-start | bytes 2838532
  3.7 3.1 %copy-start.2 = (bf16[32,1024]{1,0:T(8,128)(2,1)S(1)}, bf16[32,1024]{1,0:T(8,128)(2,1)}, u32[]{:S(2)}) copy-start(bf16[32,1024]{1,0:T(8,128)(2,1)} %resid_ref.1) | copy-start | bytes 196612
  3.7 3.1 %copy-start.3 = (bf16[32,1024]{1,0:T(8,128)(2,1)S(1)}, bf16[32,1024]{1,0:T(8,128)(2,1)}, u32[]{:S(2)}) copy-start(bf16[32,1024]{1,0:T(8,128)(2,1)} %attn_ref.1) | copy-start | bytes 196612
  3.8 3.1 %copy-start.4 = (f32[1024]{0:T(1024)S(1)}, f32[1024]{0:T(1024)}, u32[]{:S(2)}) copy-start(f32[1024]{0:T(1024)} %param.13) | copy-start | bytes 12292
  93.8 1.4 %copy-start = (f32[1024,462]{1,0:T(8,128)}, f32[1024,462]{1,0:T(8,128)S(1)}, u32[]{:S(2)}) copy-start(f32[1024,462]{1,0:T(8,128)S(1)} %get-tuple-element.32) | copy-start | bytes 5677060

commit v2 on v1

v2 whole, which is shorter than its diff:
```python
import functools

import jax
import jax.numpy as jnp
from jax import lax
from jax.experimental import pallas as pl
from jax.experimental.pallas import tpu as pltpu
from jax.sharding import PartitionSpec as P

MESH = pl.DeviceIdType.MESH
F32 = jnp.float32
BF16 = jnp.bfloat16
LEVELS = 8
ROWS = 32
NT = (((1,), (1,)), ((), ()))
NN = (((1,), (0,)), ((), ()))


def dot(a, b, dims=NN):
    return lax.dot_general(a, b, dims, preferred_element_type=F32)


def two(a):
    high = a.astype(BF16)
    return high, (a - high.astype(F32)).astype(BF16)


def exchange_kernel(
    nx,
    ny,
    nz,
    *refs,
):
    sources, refs = refs[:11], refs[11:]
    body_of_exchange(nx, ny, nz, sources, *refs)


def body_of_exchange(
    nx,
    ny,
    nz,
    sources,
    x_out,
    q_out,
    h_ref,
    head_ref,
    loss_ref,
    wheadt_ref,
    resid_ref,
    attn_ref,
    gain_ref,
    w_both,
    w_down,
    w_head_ref,
    actions_ref,
    step_ref,
    trace_ref,
    targets_ref,
    xs,
    x_mat,
    sel,
    zsum,
    meta,
    meta2,
    gpart,
    grecv,
    gfull,
    hpart,
    psum,
    rs_send,
    rs_recv,
    q_all,
    q_scaled,
    vsum,
    vsum2,
    zcoef,
    hd_part,
    hd_recv,
    hd_y,
    hd_full,
    send_sem,
    recv_sem,
    local_sem,
):
    i = lax.axis_index("dp")
    z = lax.axis_index("ffn")
    core = i % 2
    y = (i // 2) % ny
    x = i // (2 * ny)
    own, depth = resid_ref.shape
    hidden = w_down.shape[0]
    fp = q_all.shape[1]
    half = nz // 2
    tokens = own * nx * ny * 2
    chunk = tokens // nz
    share = own // nz
    bands = 16 // share
    band = depth // bands
    acts = w_head_ref.shape[0]

    def at_x(k):
        return (((x + k) % nx * ny + y) * 2 + core, z)

    def at_y(k):
        return ((x * ny + (y + k) % ny) * 2 + core, z)

    def at_xy(kx, ky):
        return (((x + kx) % nx * ny + (y + ky) % ny) * 2 + core, z)

    def at_z(k):
        return (i, (z + k) % nz)

    sibling = ((x * ny + y) * 2 + 1 - core, z)

    next_sem = [0]
    sends = []

    def copy_pair(src, dst, landing, device):
        n = next_sem[0]
        next_sem[0] += 1
        out = pltpu.make_async_remote_copy(
            src_ref=src,
            dst_ref=dst,
            send_sem=send_sem.at[n],
            recv_sem=recv_sem.at[n],
            device_id=device,
            device_id_type=MESH,
        )
        into = pltpu.make_async_remote_copy(
            src_ref=landing,
            dst_ref=landing,
            send_sem=send_sem.at[n],
            recv_sem=recv_sem.at[n],
            device_id=device,
            device_id_type=MESH,
        )
        sends.append(out)
        return out, into

    def spread(slots, me, n, at):
        arrivals = []
        for k in range(1, n):
            out, into = copy_pair(slots.at[me], slots.at[me], slots.at[(me + n - k) % n], at(k))
            out.start()
            arrivals.append(into)
        return arrivals

    def land(arrivals):
        for into in arrivals:
            into.wait_recv()

    group = 2 * x + core

    def mates():
        for k in range(nx):
            for flip in (0, 1):
                if k or flip:
                    other = core + flip - 2 * core * flip
                    device = (((x + k) % nx * ny + y) * 2 + other, z)
                    yield device, (x + k) % nx * 2 + other, (x + nx - k) % nx * 2 + other

    def spread_row(slots):
        arrivals = []
        for device, _, source in mates():
            out, into = copy_pair(slots.at[group], slots.at[group], slots.at[source], device)
            out.start()
            arrivals.append(into)
        return arrivals

    def total(slots, n):
        result = slots[0]
        for k in range(1, n):
            result = result + slots[k]
        return result

    peers = [device for device, _, _ in mates()] + [at_z(k) for k in range(1, nz)]
    peers += [at_xy(kx, ky) for kx in range(nx) for ky in range(1, ny)]
    barrier = pltpu.get_barrier_semaphore()
    for peer in peers:
        pl.semaphore_signal(barrier, inc=1, device_id=peer, device_id_type=MESH)

    places = (
        resid_ref,
        attn_ref,
        gain_ref,
        w_both.at[0],
        w_both.at[1],
        w_down,
        w_head_ref,
        actions_ref,
        step_ref,
        trace_ref,
        targets_ref,
    )
    loads = [
        pltpu.make_async_copy(src, dst, local_sem.at[n])
        for n, (src, dst) in enumerate(zip(sources, places))
    ]
    for n in (0, 1, 6, 7, 8, 9, 10, 2, 3, 4, 5):
        loads[n].start()

    row = lax.broadcasted_iota(jnp.int32, (own, chunk), 0)
    lane = lax.broadcasted_iota(jnp.int32, (own, chunk), 1)
    row8 = lax.broadcasted_iota(jnp.int32, (8, chunk), 0)
    action_row = lax.broadcasted_iota(jnp.int32, (ROWS, chunk), 0).astype(F32)

    def lanes_of(column):
        return jnp.sum(jnp.where(lane % own == row, column, 0.0), axis=0, keepdims=True)

    def rows_of(vector):
        return jnp.sum(jnp.where(lane == row, vector, 0.0), axis=1, keepdims=True)

    def column_of(vector):
        same = lane[:, :own] == row[:, :own]
        return jnp.sum(jnp.where(same, vector, 0.0), axis=1, keepdims=True)

    def stack(*vectors):
        block = jnp.zeros((8, chunk), F32)
        for n, vector in enumerate(vectors):
            block = jnp.where(row8 == n, vector, block)
        return block

    for n in (0, 1, 6, 7, 8, 9, 10, 2):
        loads[n].wait()
    cuts = nz // 4
    width = gpart.shape[2]

    def put_pieces(pieces, value):
        for p in range(nz):
            r, c = p // cuts, p % cuts
            pieces[p] = value[8 * r : 8 * r + 8, c * width : (c + 1) * width]

    def reduce_start(part, recv):
        arrivals = []
        for k in range(1, nz):
            out, into = copy_pair(
                part.at[(z + k) % nz], recv.at[z], recv.at[(z + nz - k) % nz], at_z(k)
            )
            out.start()
            arrivals.append(into)
        return arrivals

    def reduce_middle(arrivals, part, recv, full):
        recv[z] = part[z]
        land(arrivals)
        full[z] = total(recv, nz)
        return spread(full, z, nz, at_z)

    def pieces_of(full):
        rows = [
            jnp.concatenate([full[r * cuts + c] for c in range(cuts)], axis=1) for r in range(4)
        ]
        return jnp.concatenate(rows, axis=0)

    def wide(value):
        return jnp.concatenate(
            [value, jnp.zeros((ROWS, cuts * width - value.shape[1]), F32)], axis=1
        )

    summed = resid_ref[...].astype(F32) + attn_ref[...].astype(F32)
    squares = jnp.sum(summed * summed, axis=1, keepdims=True)
    eye_acts = (
        lax.broadcasted_iota(jnp.int32, (ROWS, acts), 0)
        == lax.broadcasted_iota(jnp.int32, (ROWS, acts), 1)
    ).astype(BF16)
    w_head_t = dot(eye_acts, w_head_ref[...]).astype(BF16)
    action_own = column_of(actions_ref[...].astype(F32))
    weight_own = column_of(
        jnp.power(jnp.float32(0.97), step_ref[...].astype(F32)) * trace_ref[...].astype(F32) / LEVELS
    )
    target_own = column_of(targets_ref[...])
    one_hot_own = lax.broadcasted_iota(jnp.int32, (own, ROWS), 1).astype(F32) == action_own
    scores = dot(resid_ref[...], w_head_t, NT) + dot(attn_ref[...], w_head_t, NT)
    score = jnp.sum(jnp.where(one_hot_own, scores, 0.0), axis=1, keepdims=True)
    zsum[z] = stack(lanes_of(squares), lanes_of(score))

    pl.semaphore_wait(barrier, len(peers))
    zsum_in = spread(zsum, z, nz, at_z)

    loads[5].wait()
    put_pieces(gpart, wide(dot(w_head_t, w_down[...], NT)))
    g_in = reduce_start(gpart, grecv)
    psum[...] = jnp.zeros_like(psum)
    to = lax.broadcasted_iota(jnp.int32, (chunk, 16 * chunk // share), 0)
    come = lax.broadcasted_iota(jnp.int32, (chunk, 16 * chunk // share), 1)
    for g in range(bands):
        sel[g] = (come == to // share * 16 + g * share + to % share).astype(BF16)
    wheadt_ref[...] = w_head_t

    land(zsum_in)
    zboth = total(zsum, nz)
    mean = rows_of(zboth[0:1]) / (depth * nz)
    normed = (summed * lax.rsqrt(mean + 1e-06) * gain_ref[...]).astype(BF16)

    count = nz * 16
    line = lax.broadcasted_iota(jnp.int32, (count, own), 0)
    place = line // 16
    even = half - place // 2
    offset = jnp.where(place % 2 == 0, -even, half - (place + 1) // 2)
    token = (z + offset + nz) % nz * share + line % share
    token_at = lax.broadcasted_iota(jnp.int32, (count, own), 1) == token
    packed = jnp.zeros((count, band), F32)
    for g in range(bands):
        pick = (token_at & (line % 16 // share == g)).astype(BF16)
        packed = packed + dot(pick, normed[:, g * band : (g + 1) * band])
    chip = x * ny + y
    xs[chip, core] = packed.astype(BF16).reshape(nz, 16, band)

    groups = ((0, 1), (1, 1 + half), (1 + half, nz))
    near_first = lambda n: sorted(range(n), key=lambda k: min(k, n - k))
    coming, third = {}, {}

    def send_group(n):
        places = pl.ds(groups[n][0], groups[n][1] - groups[n][0])
        coming[n] = []
        mine = xs.at[chip, core, places]
        for kx in near_first(nx):
            for ky in near_first(ny):
                if kx or ky:
                    source = (x + nx - kx) % nx * ny + (y + ny - ky) % ny
                    out, into = copy_pair(mine, mine, xs.at[source, core, places], at_xy(kx, ky))
                    out.start()
                    coming[n].append(into)

    def pass_group(n):
        places = pl.ds(groups[n][0], groups[n][1] - groups[n][0])
        land(coming[n])
        mine = xs.at[:, core, places]
        out, third[n] = copy_pair(mine, mine, xs.at[:, 1 - core, places], sibling)
        out.start()

    def gather(r):
        rows = xs[:, :, r].reshape(16 * chunk // share, band)
        for g in range(bands):
            x_mat[r, :, g * band : (g + 1) * band] = dot(sel[g], rows).astype(BF16)

    send_group(0)
    send_group(1)

    here = (row == share * z + lane % share) & (lane // share == i)

    def chunk_of(column):
        return jnp.sum(jnp.where(here, column, 0.0), axis=0, keepdims=True)

    base = rows_of(zboth[1:2]) - target_own
    meta[group] = stack(chunk_of(base), chunk_of(weight_own), chunk_of(action_own))
    meta_in = spread_row(meta)

    pass_group(0)
    send_group(2)
    third[0].wait_recv()

    hops = {(d, h): half if d == h else half - 1 for d in (0, 1) for h in (0, 1)}
    order = ((0, 0), (1, 1), (0, 1), (1, 0))
    sign = (1, -1)

    def chunk_at(offset):
        return (z + nz + offset) % nz

    loads[3].wait()
    loads[4].wait()
    waiting = {}
    cut = -(-fp // 32) * 16
    parts = (slice(0, cut), slice(cut, fp))
    for o in range(half, 0, -1):
        chosen = [dh for dh in order if hops[dh] >= o]
        if o == half - 1:
            third[1].wait_recv()
        if o == half // 2 - 1:
            third[2].wait_recv()
        if o < half:
            gather(2 * (half - o) - 1)
        gather(2 * (half - o))
        for d in (0, 1):
            r = 2 * (half - o) - 1 if d == 0 and o < half else 2 * (half - o)
            for h in (0, 1):
                if (d, h) in chosen:
                    psum[d, h, :hidden] = dot(w_both[h], x_mat[r], NT)
        for p, rows in enumerate(parts):
            for d, h in chosen:
                s = hops[d, h] - o
                value = psum[d, h, rows]
                if s > 0:
                    waiting[d, h, p].wait_recv()
                    value = value + rs_recv[d, h, s - 1, rows].astype(F32)
                rs_send[d, h, s, rows] = value.astype(BF16)
                landing = rs_recv.at[d, h, s, rows]
                out, into = copy_pair(
                    rs_send.at[d, h, s, rows], landing, landing, at_z(sign[d] % nz)
                )
                out.start()
                waiting[d, h, p] = into

        if o == half:
            land(meta_in)
            meta2[y] = total(meta, 2 * nx)
            meta_in = spread(meta2, y, ny, at_y)
            g_in = reduce_middle(g_in, gpart, grecv, gfull)
            pass_group(1)
        if o == half - 1:
            pass_group(2)

    if half < 4:
        third[2].wait_recv()
    gather(nz - 1)
    for h in (0, 1):
        psum[0, h, :hidden] = dot(w_both[h], x_mat[nz - 1], NT)
    land(meta_in)
    info = total(meta2, ny)
    land(g_in)
    g_full = jnp.transpose(pieces_of(gfull))[:fp]
    one_hot = (action_row == info[2:3]).astype(BF16)
    g_high, g_low = two(g_full)
    picked_g = dot(g_high, one_hot) + dot(g_low, one_hot)

    lanes = pl.ds(pl.multiple_of(z * chunk, chunk), chunk)
    arriving = {}

    def pass_q(d, h, s, p):
        def piece(c):
            return q_all.at[h, parts[p], pl.ds(pl.multiple_of(c * chunk, chunk), chunk)]

        if s > 0:
            arriving[d, h, p].wait_recv()
        mine = piece(chunk_at(-sign[d] * s))
        out, into = copy_pair(
            mine, mine, piece(chunk_at(-sign[d] * (s + 1))), at_z(sign[d] % nz)
        )
        out.start()
        arriving[d, h, p] = into

    def pass_on(s, p):
        for d, h in order:
            if hops[d, h] > s:
                pass_q(d, h, s, p)

    acts_of = []
    v = jnp.zeros((1, chunk), F32)
    for p, rows in enumerate(parts):
        sums = []
        for h in (0, 1):
            value = psum[0, h, rows]
            for d in (h, 1 - h):
                waiting[d, h, p].wait_recv()
                value = value + rs_recv[d, h, hops[d, h] - 1, rows].astype(F32)
            sums.append(value)
        gate, up = sums
        sg = 1.0 / (1.0 + jnp.exp(-gate))
        silu = gate * sg
        part_g = picked_g[rows]
        q_all[0, rows, lanes] = (part_g * up * sg * (1.0 + gate * (1.0 - sg))).astype(BF16)
        q_all[1, rows, lanes] = (part_g * silu).astype(BF16)
        act = (silu * up).astype(BF16).astype(F32)
        acts_of.append(act)
        v = v + jnp.sum(act * part_g, axis=0, keepdims=True)
        if p == 0:
            pass_on(0, 0)

    vsum[group] = stack(v)
    v_in = spread_row(vsum)
    pass_on(0, 1)
    act = jnp.concatenate(acts_of, axis=0)
    out_copies = []
    for r in range(nz):
        c = chunk_at(-(half - r // 2) if r % 2 == 0 else half - (r + 1) // 2)
        out = pltpu.make_async_copy(x_mat.at[r], x_out.at[c], local_sem.at[11 + r])
        out.start()
        out_copies.append(out)
    pass_on(1, 0)
    land(v_in)
    vsum2[y] = total(vsum, 2 * nx)
    v_in = spread(vsum2, y, ny, at_y)
    pass_on(1, 1)
    land(v_in)
    v_all = total(vsum2, ny)
    differ = info[0:1] + v_all[0:1]
    weight = info[1:2]
    coef = weight * differ

    fl = cuts * width
    strips = fl // 128
    row16 = lax.broadcasted_iota(jnp.int32, (16, 128), 0)
    row16_wide = lax.broadcasted_iota(jnp.int32, (16, fl), 0)

    def put_h(value):
        hpart[z, :, :fl] = value[:16].astype(BF16)
        beside = jnp.zeros((16, 128), F32)
        for n in range((acts - 16) * strips):
            a, k = 16 + n // strips, n % strips
            strip = value[a : a + 1, 128 * k : 128 * k + 128]
            beside = jnp.where(row16 == n, strip, beside)
        hpart[z, :, fl:] = beside.astype(BF16)

    def sum_h():
        value = hpart[0].astype(F32)
        for k in range(1, nz):
            value = value + hpart[k].astype(F32)
        last = jnp.zeros((16, fl), F32)
        for a in range(acts - 16):
            strip = [value[a * strips + k : a * strips + k + 1, fl:] for k in range(strips)]
            last = jnp.where(row16_wide == a, jnp.concatenate(strip, axis=1), last)
        return jnp.concatenate([value[:, :fl], last], axis=0)

    act_high, act_low = two(act * coef)
    put_h(wide(dot(one_hot, act_high, NT) + dot(one_hot, act_low, NT)))
    h_in = spread(hpart, z, nz, at_z)
    zcoef[z] = stack(coef, info[2:3], weight * differ * differ)
    zcoef_in = spread(zcoef, z, nz, at_z)
    for p in (0, 1):
        if half > 2:
            pass_on(2, p)

    land(zcoef_in)
    coef_own = jnp.zeros((own, chunk), F32)
    for c in range(nz):
        mine = (row // share == c) & (lane == i * share + row % share)
        coef_own = jnp.where(mine, zcoef[c, 0:1], coef_own)
    coef_own = jnp.sum(coef_own, axis=1, keepdims=True)
    coef_lanes = jnp.sum(
        jnp.where(lane[:, :own] == row[:, :own], coef_own, 0.0), axis=0, keepdims=True
    )
    picked = jnp.where(
        action_row[:, :own] == actions_ref[...].astype(F32), coef_lanes, 0.0
    )
    p_high, p_low = two(picked)
    head = jnp.zeros((ROWS, depth), F32)
    for ref in (resid_ref, attn_ref):
        head = head + dot(p_high, ref[...]) + dot(p_low, ref[...])
    for s in range(3, half):
        pass_on(s, 0)
        pass_on(s, 1)
    land(h_in)
    h_sum = sum_h()
    h_high, h_low = two(h_sum[:, :hidden])
    head = head + dot(h_high, w_down[...]) + dot(h_low, w_down[...])
    head_rows, piece = hd_part.shape[1:]
    for g in range(2 * nx):
        hd_part[g] = head[:head_rows, g * piece : (g + 1) * piece]
    hd_recv[group] = hd_part[group]
    hd_in = []
    for device, target, source in mates():
        out, into = copy_pair(hd_part.at[target], hd_recv.at[group], hd_recv.at[source], device)
        out.start()
        hd_in.append(into)

    def scale(c, n):
        lanes = pl.ds(pl.multiple_of(c * chunk, chunk), chunk)
        q_scaled[:, :, lanes] = (q_all[:, :, lanes].astype(F32) * zcoef[c, 0:1]).astype(BF16)
        out = pltpu.make_async_copy(
            q_scaled.at[:, :, lanes], q_out.at[:, :, lanes], local_sem.at[11 + nz + n]
        )
        out.start()
        out_copies.append(out)

    scale(z, 0)
    n = 1
    for o in range(1, half - 1):
        scale(chunk_at(o), n)
        scale(chunk_at(-o), n + 1)
        n += 2
    h_ref[...] = jnp.transpose(h_sum)
    loss = 0.5 * jnp.sum(total(zcoef, nz)[2:3], axis=1, keepdims=True) / tokens
    loss_ref[...] = jnp.broadcast_to(loss, (8, chunk))
    land(hd_in)
    hd_y[y] = total(hd_recv, 2 * nx)
    hd_in = spread(hd_y, y, ny, at_y)
    for d, h in order[2:]:
        for p in (0, 1):
            arriving[d, h, p].wait_recv()
    scale(chunk_at(half - 1), n)
    scale(chunk_at(1 - half), n + 1)
    for d, h in order[:2]:
        for p in (0, 1):
            arriving[d, h, p].wait_recv()
    scale(chunk_at(half), n + 2)
    land(hd_in)
    hd_full[group] = total(hd_y, ny)
    land(spread_row(hd_full))
    head_ref[...] = jnp.concatenate([hd_full[g] for g in range(2 * nx)], axis=1)
    for out in sends:
        out.wait_send()
    for out in out_copies:
        out.wait()


def grads_kernel(x_ref, q_ref, h_ref, head_ref, loss_ref, wheadt_ref, gg, gu, gd, gh, loss):
    hidden, acts = gd.shape[0], gh.shape[0]
    fp = q_ref.shape[1]
    block = x_ref[...]
    gg[...] = dot(q_ref[0], block)[:hidden]
    gu[...] = dot(q_ref[1], block)[:hidden]
    h_high, h_low = two(h_ref[:fp])
    head_t = wheadt_ref[...]
    gd[...] = (dot(h_high, head_t) + dot(h_low, head_t))[:hidden]
    gh[...] = head_ref[:acts]
    loss[0, 0] = loss_ref[0, 0]


def body(
    nx,
    ny,
    nz,
    resid,
    attn_out,
    norm_gain,
    w_gate,
    w_up,
    w_down,
    w_head,
    actions,
    step_index,
    trace_code,
    targets,
):
    own, depth = resid.shape
    hidden = w_down.shape[0]
    acts = w_head.shape[1]
    fp = -(-hidden // 16) * 16
    fl = -(-hidden // 128) * 128
    tokens = own * nx * ny * 2
    chunk = tokens // nz
    share = own // nz
    bands = 16 // share
    half = nz // 2
    cuts = nz // 4
    head_rows = -(-acts // 8) * 8
    vmem = pl.BlockSpec(memory_space=pltpu.VMEM)
    anywhere = pl.BlockSpec(memory_space=pl.ANY)
    shape = jax.ShapeDtypeStruct
    n_sems = (
        3 * nx * ny + 4 * (2 * nx - 1) + 3 * (ny - 1)
        + 5 * (nz - 1)
        + 4 * 2 * (2 * half - 1)
    )
    pieces = pltpu.VMEM((nz, 8, fl // cuts), F32)
    row_slots = pltpu.VMEM((2 * nx, 8, chunk), F32)
    y_slots = pltpu.VMEM((ny, 8, chunk), F32)
    head_row = pltpu.VMEM((2 * nx, head_rows, depth // (2 * nx)), F32)
    x_out, q, h, head, loss, w_head_t = pl.pallas_call(
        functools.partial(exchange_kernel, nx, ny, nz),
        out_shape=(
            shape((nz, chunk, depth), BF16),
            shape((2, fp, tokens), BF16),
            shape((fl, ROWS), F32),
            shape((head_rows, depth), F32),
            shape((8, chunk), F32),
            shape((ROWS, depth), BF16),
        ),
        in_specs=[pl.BlockSpec(memory_space=pltpu.HBM)] * 11,
        out_specs=(anywhere, anywhere, vmem, vmem, vmem, vmem),
        scratch_shapes=[
            pltpu.VMEM((own, depth), BF16),
            pltpu.VMEM((own, depth), BF16),
            pltpu.VMEM((1, depth), F32),
            pltpu.VMEM((2, hidden, depth), BF16),
            pltpu.VMEM((hidden, depth), BF16),
            pltpu.VMEM((acts, depth), BF16),
            pltpu.VMEM((1, own), jnp.int32),
            pltpu.VMEM((1, own), jnp.int32),
            pltpu.VMEM((1, own), jnp.int32),
            pltpu.VMEM((1, own), F32),
            pltpu.VMEM((nx * ny, 2, nz, 16, depth // bands), BF16),
            pltpu.VMEM((nz, chunk, depth), BF16),
            pltpu.VMEM((bands, chunk, 16 * chunk // share), BF16),
            pltpu.VMEM((nz, 8, chunk), F32),
            row_slots,
            y_slots,
            pieces,
            pieces,
            pieces,
            pltpu.VMEM((nz, 16, fl + 128), BF16),
            pltpu.VMEM((2, 2, fp, chunk), F32),
            pltpu.VMEM((2, 2, half, fp, chunk), BF16),
            pltpu.VMEM((2, 2, half, fp, chunk), BF16),
            pltpu.VMEM((2, fp, tokens), BF16),
            pltpu.VMEM((2, fp, tokens), BF16),
            row_slots,
            y_slots,
            pltpu.VMEM((nz, 8, chunk), F32),
            head_row,
            head_row,
            pltpu.VMEM((ny, head_rows, depth // (2 * nx)), F32),
            head_row,
            pltpu.SemaphoreType.DMA((n_sems,)),
            pltpu.SemaphoreType.DMA((n_sems,)),
            pltpu.SemaphoreType.DMA((11 + 2 * nz,)),
        ],
        compiler_params=pltpu.CompilerParams(
            collective_id=0, has_side_effects=True, vmem_limit_bytes=60 * 1024 * 1024
        ),
        name="exchange",
    )(
        resid,
        attn_out,
        norm_gain.reshape(1, depth),
        w_gate.T,
        w_up.T,
        w_down,
        w_head.T,
        actions.reshape(1, own),
        step_index.reshape(1, own),
        trace_code.reshape(1, own),
        targets.reshape(1, own),
    )

    tile = min(256, depth)
    grad_gate, grad_up, grad_down, grad_head, loss = pl.pallas_call(
        grads_kernel,
        grid=(depth // tile,),
        out_shape=(
            shape((hidden, depth), F32),
            shape((hidden, depth), F32),
            shape((hidden, depth), F32),
            shape((acts, depth), F32),
            shape((1, 1), F32),
        ),
        in_specs=[
            pl.BlockSpec((tokens, tile), lambda n: (0, n)),
            pl.BlockSpec((2, fp, tokens), lambda n: (0, 0, 0)),
            pl.BlockSpec((fl, ROWS), lambda n: (0, 0)),
            pl.BlockSpec((head_rows, tile), lambda n: (0, n)),
            pl.BlockSpec((8, chunk), lambda n: (0, 0)),
            pl.BlockSpec((ROWS, tile), lambda n: (0, n)),
        ],
        out_specs=(
            pl.BlockSpec((hidden, tile), lambda n: (0, n)),
            pl.BlockSpec((hidden, tile), lambda n: (0, n)),
            pl.BlockSpec((hidden, tile), lambda n: (0, n)),
            pl.BlockSpec((acts, tile), lambda n: (0, n)),
            pl.BlockSpec((1, 1), lambda n: (0, 0), memory_space=pltpu.SMEM),
        ),
        compiler_params=pltpu.CompilerParams(vmem_limit_bytes=60 * 1024 * 1024),
        name="weight_grads",
    )(x_out.reshape(tokens, depth), q, h, head, loss, w_head_t)
    return grad_gate.T, grad_up.T, grad_down, grad_head.T, loss.reshape(())


def build(mesh, nx, ny):
    nz = mesh.shape["ffn"]
    in_specs = (
        P("dp", "ffn"),
        P("dp", "ffn"),
        P("ffn"),
        P("ffn", "dp"),
        P("ffn", "dp"),
        P("dp", "ffn"),
        P("ffn", None),
        P("dp"),
        P("dp"),
        P("dp"),
        P("dp"),
    )
    out_specs = (P("ffn", "dp"), P("ffn", "dp"), P("dp", "ffn"), P("ffn", None), P())
    return jax.shard_map(
        functools.partial(body, nx, ny, nz),
        mesh=mesh,
        in_specs=in_specs,
        out_specs=out_specs,
        check_vma=False,
    )


def solution(mesh):
    return build(mesh, 4, 4)
```

time: 101 us -> 91 us (0.901)
  local copies, waits for them, and re-layouts: 10.9 us -> 0 us
  Pallas kernels: 86.9 us -> 90.2 us
  other arithmetic: 2.01 us -> 0 us
    unnamed x16 -> x0, local copies, waits for them, and re-layouts: 10.8 us -> none
    pallas_call x1, Pallas kernels: 4.37 us -> 6.68 us  [body(): pl.pallas_call(grads_kernel, grid=(depth // tile,), out_shape=(shape((hid...]
    another operation x3 -> x0, other arithmetic: 2.01 us -> none  [body(): info = jnp.stack([weight, targets, actions.astype(F32)], axis=1)]
where the time goes in v2:
time: 91 us; the launch traced here: 90.8 us
  Pallas kernels  90.2 us (99%)
    pallas_call x1, Pallas kernels, body(): pl.pallas_call(functools.partial(exchange_kernel, nx, ny, nz), out_shape=...  83.5 us
    pallas_call x1, Pallas kernels, body(): pl.pallas_call(grads_kernel, grid=(depth // tile,), out_shape=(shape((hid...  6.68 us

profile of v2, /device:TPU:1, one launch (start us, length us, event | category | flops | bytes accessed | tf_op | source)
XLA Modules:
  0.0 90.8 jit_solution(5017246336889970949)
XLA Ops:
  0.6 83.5 %exchange.1 = (bf16[8,128,1024]{2,1,0:T(8,128)(2,1)}, bf16[2,464,1024]{2,1,0:T(8,128)(2,1)}, f32[512,32]{1,0:T(8,128)}, f32[24,1024]{1,0:T(8,128)}, f32[8,128]{1,0:T(8,128)}, /*index=5*/bf16[32,1024]{1,0:T(8,128)(2,1)}) custom-call(bf16[32,1024]{1,0:T(8,128)(2,1)} %refs_0_.1, bf16[32,1024]{1,0:T(8,128)(2,1)} %refs_1_.1, f32[1,1024]{1,0:T(1,128)} %bitcast.17, ...), custom_call_target="tpu_custom_call" | custom-call | tf_op jit(solution)/shard_map/exchange/pallas_call | solution.py:639
  84.1 6.7 %weight_grads.1 = (f32[462,1024]{1,0:T(8,128)}, f32[462,1024]{1,0:T(8,128)}, f32[462,1024]{1,0:T(8,128)}, f32[18,1024]{1,0:T(8,128)}, f32[1,1]{1,0:T(1,128)}) custom-call(bf16[1024,1024]{1,0:T(8,128)(2,1)} %bitcast.13, bf16[2,464,1024]{2,1,0:T(8,128)(2,1)} %get-tuple-element.17.q_ref, f32[512,32]{1,0:T(8,128)} %get-tuple-element.18.h_ref, ...), custom_call_target="tpu_custom_call" | custom-call | tf_op jit(solution)/shard_map/weight_grads/pallas_call | solution.py:707

commit v3 on v2

--- a/solution.py
+++ b/solution.py
@@ -280,17 +280,7 @@
     loads[5].wait()
     put_pieces(gpart, wide(dot(w_head_t, w_down[...], NT)))
     g_in = reduce_start(gpart, grecv)
-    psum[...] = jnp.zeros_like(psum)
-    to = lax.broadcasted_iota(jnp.int32, (chunk, 16 * chunk // share), 0)
-    come = lax.broadcasted_iota(jnp.int32, (chunk, 16 * chunk // share), 1)
-    for g in range(bands):
-        sel[g] = (come == to // share * 16 + g * share + to % share).astype(BF16)
     wheadt_ref[...] = w_head_t
-
-    land(zsum_in)
-    zboth = total(zsum, nz)
-    mean = rows_of(zboth[0:1]) / (depth * nz)
-    normed = (summed * lax.rsqrt(mean + 1e-06) * gain_ref[...]).astype(BF16)
 
     count = nz * 16
     line = lax.broadcasted_iota(jnp.int32, (count, own), 0)
@@ -299,10 +289,16 @@
     offset = jnp.where(place % 2 == 0, -even, half - (place + 1) // 2)
     token = (z + offset + nz) % nz * share + line % share
     token_at = lax.broadcasted_iota(jnp.int32, (count, own), 1) == token
+    picks = [(token_at & (line % 16 // share == g)).astype(BF16) for g in range(bands)]
+
+    land(zsum_in)
+    zboth = total(zsum, nz)
+    mean = rows_of(zboth[0:1]) / (depth * nz)
+    normed = (summed * lax.rsqrt(mean + 1e-06) * gain_ref[...]).astype(BF16)
+
     packed = jnp.zeros((count, band), F32)
     for g in range(bands):
-        pick = (token_at & (line % 16 // share == g)).astype(BF16)
-        packed = packed + dot(pick, normed[:, g * band : (g + 1) * band])
+        packed = packed + dot(picks[g], normed[:, g * band : (g + 1) * band])
     chip = x * ny + y
     xs[chip, core] = packed.astype(BF16).reshape(nz, 16, band)
 
@@ -336,6 +332,11 @@
 
     send_group(0)
     send_group(1)
+    psum[...] = jnp.zeros_like(psum)
+    to = lax.broadcasted_iota(jnp.int32, (chunk, 16 * chunk // share), 0)
+    come = lax.broadcasted_iota(jnp.int32, (chunk, 16 * chunk // share), 1)
+    for g in range(bands):
+        sel[g] = (come == to // share * 16 + g * share + to % share).astype(BF16)
 
     here = (row == share * z + lane % share) & (lane // share == i)
 
@@ -390,13 +391,13 @@
                 )
                 out.start()
                 waiting[d, h, p] = into
-
-        if o == half:
-            land(meta_in)
-            meta2[y] = total(meta, 2 * nx)
-            meta_in = spread(meta2, y, ny, at_y)
-            g_in = reduce_middle(g_in, gpart, grecv, gfull)
-            pass_group(1)
+            if o == half and p == 0:
+                land(meta_in)
+                meta2[y] = total(meta, 2 * nx)
+                meta_in = spread(meta2, y, ny, at_y)
+                g_in = reduce_middle(g_in, gpart, grecv, gfull)
+                pass_group(1)
+
         if o == half - 1:
             pass_group(2)
 
@@ -526,9 +527,6 @@
     head = jnp.zeros((ROWS, depth), F32)
     for ref in (resid_ref, attn_ref):
         head = head + dot(p_high, ref[...]) + dot(p_low, ref[...])
-    for s in range(3, half):
-        pass_on(s, 0)
-        pass_on(s, 1)
     land(h_in)
     h_sum = sum_h()
     h_high, h_low = two(h_sum[:, :hidden])
@@ -552,18 +550,29 @@
         out.start()
         out_copies.append(out)
 
+    if half > 3:
+        pass_on(3, 0)
     scale(z, 0)
+    land(hd_in)
+    hd_y[y] = total(hd_recv, 2 * nx)
+    hd_in = spread(hd_y, y, ny, at_y)
+    if half > 3:
+        pass_on(3, 1)
     n = 1
-    for o in range(1, half - 1):
+    if half > 2:
+        scale(chunk_at(1), n)
+        scale(chunk_at(-1), n + 1)
+        n += 2
+    land(hd_in)
+    hd_full[group] = total(hd_y, ny)
+    hd_in = spread_row(hd_full)
+    for o in range(2, half - 1):
         scale(chunk_at(o), n)
         scale(chunk_at(-o), n + 1)
         n += 2
     h_ref[...] = jnp.transpose(h_sum)
     loss = 0.5 * jnp.sum(total(zcoef, nz)[2:3], axis=1, keepdims=True) / tokens
     loss_ref[...] = jnp.broadcast_to(loss, (8, chunk))
-    land(hd_in)
-    hd_y[y] = total(hd_recv, 2 * nx)
-    hd_in = spread(hd_y, y, ny, at_y)
     for d, h in order[2:]:
         for p in (0, 1):
             arriving[d, h, p].wait_recv()
@@ -574,8 +583,6 @@
             arriving[d, h, p].wait_recv()
     scale(chunk_at(half), n + 2)
     land(hd_in)
-    hd_full[group] = total(hd_y, ny)
-    land(spread_row(hd_full))
     head_ref[...] = jnp.concatenate([hd_full[g] for g in range(2 * nx)], axis=1)
     for out in sends:
         out.wait_send()

time: 91 us -> 87.5 us (0.962)
  Pallas kernels: 90.2 us -> 86.7 us
    pallas_call x1, Pallas kernels: 83.5 us -> 80 us  [body(): pl.pallas_call(functools.partial(exchange_kernel, nx, ny, nz), out_shape=...]
where the time goes in v3:
time: 87.5 us; the launch traced here: 87.3 us
  Pallas kernels  86.7 us (99%)
    pallas_call x1, Pallas kernels, body(): pl.pallas_call(functools.partial(exchange_kernel, nx, ny, nz), out_shape=...  80 us
    pallas_call x1, Pallas kernels, body(): pl.pallas_call(grads_kernel, grid=(depth // tile,), out_shape=(shape((hid...  6.68 us

profile of v3, /device:TPU:1, one launch (start us, length us, event | category | flops | bytes accessed | tf_op | source)
XLA Modules:
  0.0 87.3 jit_solution(459907279253926400)
XLA Ops:
  0.6 80.0 %exchange.1 = (bf16[8,128,1024]{2,1,0:T(8,128)(2,1)}, bf16[2,464,1024]{2,1,0:T(8,128)(2,1)}, f32[512,32]{1,0:T(8,128)}, f32[24,1024]{1,0:T(8,128)}, f32[8,128]{1,0:T(8,128)}, /*index=5*/bf16[32,1024]{1,0:T(8,128)(2,1)}) custom-call(bf16[32,1024]{1,0:T(8,128)(2,1)} %refs_0_.1, bf16[32,1024]{1,0:T(8,128)(2,1)} %refs_1_.1, f32[1,1024]{1,0:T(1,128)} %bitcast.17, ...), custom_call_target="tpu_custom_call" | custom-call | tf_op jit(solution)/shard_map/exchange/pallas_call | solution.py:646
  80.6 6.7 %weight_grads.1 = (f32[462,1024]{1,0:T(8,128)}, f32[462,1024]{1,0:T(8,128)}, f32[462,1024]{1,0:T(8,128)}, f32[18,1024]{1,0:T(8,128)}, f32[1,1]{1,0:T(1,128)}) custom-call(bf16[1024,1024]{1,0:T(8,128)(2,1)} %bitcast.13, bf16[2,464,1024]{2,1,0:T(8,128)(2,1)} %get-tuple-element.17.q_ref, f32[512,32]{1,0:T(8,128)} %get-tuple-element.18.h_ref, ...), custom_call_target="tpu_custom_call" | custom-call | tf_op jit(solution)/shard_map/weight_grads/pallas_call | solution.py:714

commit v4 on v3

--- a/solution.py
+++ b/solution.py
@@ -552,20 +552,20 @@
 
     if half > 3:
         pass_on(3, 0)
-    scale(z, 0)
     land(hd_in)
     hd_y[y] = total(hd_recv, 2 * nx)
     hd_in = spread(hd_y, y, ny, at_y)
     if half > 3:
         pass_on(3, 1)
+    scale(z, 0)
+    land(hd_in)
+    hd_full[group] = total(hd_y, ny)
+    hd_in = spread_row(hd_full)
     n = 1
     if half > 2:
         scale(chunk_at(1), n)
         scale(chunk_at(-1), n + 1)
         n += 2
-    land(hd_in)
-    hd_full[group] = total(hd_y, ny)
-    hd_in = spread_row(hd_full)
     for o in range(2, half - 1):
         scale(chunk_at(o), n)
         scale(chunk_at(-o), n + 1)
@@ -710,7 +710,7 @@
         targets.reshape(1, own),
     )
 
-    tile = min(256, depth)
+    tile = min(512, depth)
     grad_gate, grad_up, grad_down, grad_head, loss = pl.pallas_call(
         grads_kernel,
         grid=(depth // tile,),

time: 87.5 us -> 86.7 us (level)
  no operation moved by 1% of the time
where the time goes in v4:
time: 86.7 us; the launch traced here: 86.5 us
  Pallas kernels  85.9 us (99%)
    pallas_call x1, Pallas kernels, body(): pl.pallas_call(functools.partial(exchange_kernel, nx, ny, nz), out_shape=...  80 us
    pallas_call x1, Pallas kernels, body(): pl.pallas_call(grads_kernel, grid=(depth // tile,), out_shape=(shape((hid...  5.91 us

profile of v4, /device:TPU:1, one launch (start us, length us, event | category | flops | bytes accessed | tf_op | source)
XLA Modules:
  0.0 86.5 jit_solution(9227386150780873418)
XLA Ops:
  0.6 80.0 %exchange.1 = (bf16[8,128,1024]{2,1,0:T(8,128)(2,1)}, bf16[2,464,1024]{2,1,0:T(8,128)(2,1)}, f32[512,32]{1,0:T(8,128)}, f32[24,1024]{1,0:T(8,128)}, f32[8,128]{1,0:T(8,128)}, /*index=5*/bf16[32,1024]{1,0:T(8,128)(2,1)}) custom-call(bf16[32,1024]{1,0:T(8,128)(2,1)} %refs_0_.1, bf16[32,1024]{1,0:T(8,128)(2,1)} %refs_1_.1, f32[1,1024]{1,0:T(1,128)} %bitcast.17, ...), custom_call_target="tpu_custom_call" | custom-call | tf_op jit(solution)/shard_map/exchange/pallas_call | solution.py:646
  80.6 5.9 %weight_grads.1 = (f32[462,1024]{1,0:T(8,128)}, f32[462,1024]{1,0:T(8,128)}, f32[462,1024]{1,0:T(8,128)}, f32[18,1024]{1,0:T(8,128)}, f32[1,1]{1,0:T(1,128)}) custom-call(bf16[1024,1024]{1,0:T(8,128)(2,1)} %bitcast.13, bf16[2,464,1024]{2,1,0:T(8,128)(2,1)} %get-tuple-element.17.q_ref, f32[512,32]{1,0:T(8,128)} %get-tuple-element.18.h_ref, ...), custom_call_target="tpu_custom_call" | custom-call | tf_op jit(solution)/shard_map/weight_grads/pallas_call | solution.py:714
